TPU v7x, 128 devices: a whole 4x4x4 slice. The times are simulated.
128 devices in a mesh: patch: 16 (over z, x), exp: 8 (over y, core).
Axes of the slice: x: 4, y: 4, z: 4, core: 2. Of those that a mesh axis runs over, the one named last changes fastest.
Arguments:
- sky_model: float32 [16, 8, 6, 256, 256], P('patch', 'exp'), may hold values from -6 to 6
- stamp_pixels: bfloat16 [16384, 256, 256], P(('patch', 'exp')), may hold values from -6 to 6
- stamp_patch: int32 [16384, 1], P(('patch', 'exp')), may hold values from 0 to 15; in each aligned block of 128 rows (0 to 127, 128 to 255, ...) at most 12 rows name the same one
- stamp_band: int32 [16384], P(('patch', 'exp')), may hold values from 0 to 5
- psf_taps: bfloat16 [16384, 2, 21], P(('patch', 'exp')), may hold values from 0.019897461 to 0.19921875
- stamp_gain: bfloat16 [16384], P(('patch', 'exp')), may hold values from 0.5 to 2
- stamp_weight: bfloat16 [16384], P(('patch', 'exp')), may hold values from 0.25 to 4
Outputs:
- new_model: float32 [16, 8, 6, 256, 256], P('patch', 'exp')
- step_rms: float32 [], replicated
Inputs may be any that keep to these rules, and one draw needn't show every extreme that they name: `stamp_patch`: among the stamps of one device no patch is named by more than 12 stamps, a bound that some block reaches.
All inputs are finite; a program needn't handle non-finite values.
Results may differ from a plain program's by a relative error of at most 0.013.
Values may be sent and summed in bfloat16 or wider, within the bound.
A program may use at most 192 MiB of HBM per device.

v0:
```python
import jax
import jax.numpy as jnp
from jax import lax
from jax.sharding import PartitionSpec as P

step_rate = 0.2


def banded_matrices(tap_values, tile_size):
    tap_length = tap_values.shape[-1]
    half_width = (tap_length - 1) // 2
    pixel_index = jnp.arange(tile_size, dtype=jnp.int32)
    offset = pixel_index[None, :] - pixel_index[:, None] + half_width
    tap_table = (
        offset[None, :, :] == jnp.arange(tap_length, dtype=jnp.int32)[:, None, None]
    ).astype(jnp.bfloat16)
    return jnp.einsum(
        "sk,kij->sij", tap_values, tap_table, preferred_element_type=jnp.float32
    ).astype(jnp.bfloat16)


def stamp_adjoint(tile_sel, pixels, tap_values, gain_rows, weight_rows):
    tile_size = pixels.shape[-1]
    row_kernel = banded_matrices(tap_values[:, 0], tile_size)
    col_kernel = banded_matrices(tap_values[:, 1], tile_size)
    blurred = jnp.einsum(
        "sab,scb->sac", tile_sel, col_kernel, preferred_element_type=jnp.float32
    ).astype(jnp.bfloat16)
    gain_wide = gain_rows.astype(jnp.float32)[:, None, None]
    predicted = gain_wide * jnp.einsum(
        "sab,sbc->sac", row_kernel, blurred, preferred_element_type=jnp.float32
    )
    residual = (
        weight_rows.astype(jnp.float32)[:, None, None] * (predicted - pixels.astype(jnp.float32))
    ).astype(jnp.bfloat16)
    backward = jnp.einsum(
        "sba,sbc->sac", row_kernel, residual, preferred_element_type=jnp.float32
    ).astype(jnp.bfloat16)
    return gain_wide * jnp.einsum(
        "sab,sbc->sac", backward, col_kernel, preferred_element_type=jnp.float32
    )


def per_device(
    sky_model, stamp_pixels, stamp_patch, stamp_band, psf_taps, stamp_gain, stamp_weight
):
    band_count = sky_model.shape[2]
    tile_size = sky_model.shape[-1]
    stamp_count = stamp_pixels.shape[0]
    tap_length = psf_taps.shape[-1]
    block_rows = 32
    model_half = sky_model.astype(jnp.bfloat16)
    patches = lax.axis_size("patch")
    gathered = lax.all_gather(model_half, "patch", axis=0, tiled=True)
    key_count = gathered.shape[0] * band_count
    flat_tiles = gathered.reshape(key_count, tile_size, tile_size)
    tile_keys = stamp_patch[:, 0] * band_count + stamp_band
    block_count = stamp_count // block_rows
    block_inputs = (
        stamp_pixels.reshape(block_count, block_rows, tile_size, tile_size),
        tile_keys.reshape(block_count, block_rows),
        psf_taps.reshape(block_count, block_rows, 2, tap_length),
        stamp_gain.reshape(block_count, block_rows),
        stamp_weight.reshape(block_count, block_rows),
    )

    def source_block(running, block_parts):
        pixels, keys_block, tap_values, gain_rows, weight_rows = block_parts
        tile_sel = jnp.take(flat_tiles, keys_block, axis=0)
        adjoint = stamp_adjoint(tile_sel, pixels, tap_values, gain_rows, weight_rows)
        return (running.at[keys_block].add(adjoint), None)

    result = lax.scan(
        source_block, jnp.zeros((key_count, tile_size, tile_size), jnp.float32), block_inputs
    )
    gradient = lax.psum_scatter(
        result[0].reshape(gathered.shape).astype(jnp.bfloat16),
        "patch",
        scatter_dimension=0,
        tiled=True,
    ).astype(jnp.float32)
    step_field = step_rate * gradient
    new_model = sky_model - step_field
    square_sum = lax.psum(jnp.sum(step_field * step_field), ("patch", "exp"))
    entry_count = patches * lax.axis_size("exp") * band_count * tile_size * tile_size
    step_rms = jnp.sqrt(square_sum / entry_count + 1e-06)
    return (new_model, step_rms)


def solution(mesh):
    return jax.shard_map(
        per_device,
        mesh=mesh,
        in_specs=(
            P("patch", "exp", None, None, None),
            P(("patch", "exp"), None, None),
            P(("patch", "exp"), None),
            P(("patch", "exp")),
            P(("patch", "exp"), None, None),
            P(("patch", "exp")),
            P(("patch", "exp")),
        ),
        out_specs=(P("patch", "exp", None, None, None), P()),
        check_vma=False,
    )
```

profile of v0, /device:TPU:1, one launch (start us, length us, event | category | flops | bytes accessed | tf_op | source)
XLA Modules:
  0.0 557.4 jit_solution(9071368639380420495)
XLA Ops:
  12.7 91.4 %all-gather.2.cloned.1.call-done = bf16[16,1,6,256,256]{4,3,2,1,0:T(8,128)(2,1)} async-done(((bf16[1,1,6,256,256]{4,3,2,1,0:T(8,128)(2,1)}), bf16[16,1,6,256,256]{4,3,2,1,0:T(8,128)(2,1)}) %all-gather.2.cloned.1.call-update) | async-done | bytes 12582928 | tf_op jit(solution)/shard_map/all_gather | solution.py:54
  104.1 11.4 %broadcast_in_dim.12 = f32[96,256,256]{2,1,0:T(8,128)} broadcast(f32[]{:T(128)} %constant.24.clone.1), dimensions={} | broadcast | bytes 25165828 | tf_op jit(solution)/shard_map/broadcast_in_dim | solution.py:74
  115.5 258.0 %while.10 = (s32[]{:T(128)}, f32[96,256,256]{2,1,0:T(8,128)}, s32[4,32]{1,0:T(4,128)S(1)}, bf16[4,32]{1,0:T(4,128)(2,1)S(1)}, bf16[4,32,2,21]{1,3,2,0:T(8,128)(2...) while((s32[]{:T(128)}, f32[96,256,256]{2,1,0:T(8,128)}, ...), condition=%wide.region_2.3_spmd, body=%wide.region_0.2_spmd.sunk | while | flops 4494984704 | bytes 135027696 | solution.py:73
  115.6 7.3 %gather_fusion = bf16[32,256,256]{2,1,0:T(8,128)(2,1)} fusion(bf16[96,256,256]{2,1,0:T(8,128)(2,1)} %get-tuple-element.158, s32[1024]{0:T(1024)S(1)} %pad_clamp_fusion.2), kind=kCustom, calls=%fused_computation.clone.1 | custom fusion | bytes 8388736 | tf_op jit(solution)/shard_map/while/body/eval_jaxpr/jit(_take)/gather | solution.py:69
  125.2 5.0 fusion.70
  130.2 3.3 fusion.69
  133.5 7.5 %copy.28 = bf16[32,256,256]{1,2,0:T(8,128)(2,1)} copy(bf16[32,256,256]{2,0,1:T(8,128)(2,1)} %fusion.69) | data formatting | bytes 8388608 | tf_op jit(solution)/shard_map/while/body/eval_jaxpr/convert_element_type | solution.py:19
  141.0 10.6 %fusion.71 = bf16[32,256,256]{2,1,0:T(8,128)(2,1)} fusion(bf16[32,256,256]{1,2,0:T(8,128)(2,1)} %copy.28, bf16[4,32,256,256]{3,2,1,0:T(8,128)(2,1)} %get-tuple-element.159, s32[]{:T(128)S(6)} %copy.32, f32[32]{0:T(128)S(1)} %get-tuple-element.133, f32[32]{0:T(128)S(1)} %get-tuple-element.132, bf16[32,256,256]{2,1,0:T(8,128)(2,1)} %fusion.70), kind=kOutput, calls=%fused_computation.8.clone.1 | convolution fusion | flops 2157969408 | bytes 20971780 | tf_op jit(solution)/shard_map/while/body/eval_jaxpr/sba,sbc->sac/dot_general | solution.py:36
  151.7 9.6 %broadcast_multiply_fusion.2 = f32[32,256,256]{2,1,0:T(8,128)} fusion(f32[32]{0:T(128)S(1)} %get-tuple-element.132, bf16[32,256,256]{2,0,1:T(8,128)(2,1)} %copy-done, bf16[32,256,256]{2,1,0:T(8,128)(2,1)} %fusion.71), kind=kOutput, calls=%fused_computation.18.clone.1 | convolution fusion | flops 1075838976 | bytes 16777344 | tf_op jit(solution)/shard_map/while/body/eval_jaxpr/sab,sbc->sac/dot_general | solution.py:39
  161.2 18.8 %scatter_fusion = f32[96,256,256]{2,1,0:T(8,128)} fusion(f32[96,256,256]{2,1,0:T(8,128)} %get-tuple-element.144, s32[32]{0:T(128)S(1)} %fusion.66, f32[32,256,256]{2,1,0:T(8,128)} %broadcast_multiply_fusion.2), kind=kCustom, calls=%fused_computation.1.clone.1 | custom fusion | flops 2097152 | bytes 25165952 | tf_op jit(solution)/shard_map/while/body/eval_jaxpr/scatter-add | solution.py:71
  180.1 7.3 %gather_fusion = bf16[32,256,256]{2,1,0:T(8,128)(2,1)} fusion(bf16[96,256,256]{2,1,0:T(8,128)(2,1)} %get-tuple-element.158, s32[1024]{0:T(1024)S(1)} %pad_clamp_fusion.2), kind=kCustom, calls=%fused_computation.clone.1 | custom fusion | bytes 8388736 | tf_op jit(solution)/shard_map/while/body/eval_jaxpr/jit(_take)/gather | solution.py:69
  189.7 5.0 fusion.70
  198.0 7.5 %copy.28 = bf16[32,256,256]{1,2,0:T(8,128)(2,1)} copy(bf16[32,256,256]{2,0,1:T(8,128)(2,1)} %fusion.69) | data formatting | bytes 8388608 | tf_op jit(solution)/shard_map/while/body/eval_jaxpr/convert_element_type | solution.py:19
  205.5 10.6 %fusion.71 = bf16[32,256,256]{2,1,0:T(8,128)(2,1)} fusion(bf16[32,256,256]{1,2,0:T(8,128)(2,1)} %copy.28, bf16[4,32,256,256]{3,2,1,0:T(8,128)(2,1)} %get-tuple-element.159, s32[]{:T(128)S(6)} %copy.32, f32[32]{0:T(128)S(1)} %get-tuple-element.133, f32[32]{0:T(128)S(1)} %get-tuple-element.132, bf16[32,256,256]{2,1,0:T(8,128)(2,1)} %fusion.70), kind=kOutput, calls=%fused_computation.8.clone.1 | convolution fusion | flops 2157969408 | bytes 20971780 | tf_op jit(solution)/shard_map/while/body/eval_jaxpr/sba,sbc->sac/dot_general | solution.py:36
  216.1 9.6 %broadcast_multiply_fusion.2 = f32[32,256,256]{2,1,0:T(8,128)} fusion(f32[32]{0:T(128)S(1)} %get-tuple-element.132, bf16[32,256,256]{2,0,1:T(8,128)(2,1)} %copy-done, bf16[32,256,256]{2,1,0:T(8,128)(2,1)} %fusion.71), kind=kOutput, calls=%fused_computation.18.clone.1 | convolution fusion | flops 1075838976 | bytes 16777344 | tf_op jit(solution)/shard_map/while/body/eval_jaxpr/sab,sbc->sac/dot_general | solution.py:39
  225.7 18.9 %scatter_fusion = f32[96,256,256]{2,1,0:T(8,128)} fusion(f32[96,256,256]{2,1,0:T(8,128)} %get-tuple-element.144, s32[32]{0:T(128)S(1)} %fusion.66, f32[32,256,256]{2,1,0:T(8,128)} %broadcast_multiply_fusion.2), kind=kCustom, calls=%fused_computation.1.clone.1 | custom fusion | flops 2097152 | bytes 25165952 | tf_op jit(solution)/shard_map/while/body/eval_jaxpr/scatter-add | solution.py:71
  244.7 7.3 %gather_fusion = bf16[32,256,256]{2,1,0:T(8,128)(2,1)} fusion(bf16[96,256,256]{2,1,0:T(8,128)(2,1)} %get-tuple-element.158, s32[1024]{0:T(1024)S(1)} %pad_clamp_fusion.2), kind=kCustom, calls=%fused_computation.clone.1 | custom fusion | bytes 8388736 | tf_op jit(solution)/shard_map/while/body/eval_jaxpr/jit(_take)/gather | solution.py:69
  254.2 5.0 fusion.70
  262.5 7.5 %copy.28 = bf16[32,256,256]{1,2,0:T(8,128)(2,1)} copy(bf16[32,256,256]{2,0,1:T(8,128)(2,1)} %fusion.69) | data formatting | bytes 8388608 | tf_op jit(solution)/shard_map/while/body/eval_jaxpr/convert_element_type | solution.py:19
  270.0 10.6 %fusion.71 = bf16[32,256,256]{2,1,0:T(8,128)(2,1)} fusion(bf16[32,256,256]{1,2,0:T(8,128)(2,1)} %copy.28, bf16[4,32,256,256]{3,2,1,0:T(8,128)(2,1)} %get-tuple-element.159, s32[]{:T(128)S(6)} %copy.32, f32[32]{0:T(128)S(1)} %get-tuple-element.133, f32[32]{0:T(128)S(1)} %get-tuple-element.132, bf16[32,256,256]{2,1,0:T(8,128)(2,1)} %fusion.70), kind=kOutput, calls=%fused_computation.8.clone.1 | convolution fusion | flops 2157969408 | bytes 20971780 | tf_op jit(solution)/shard_map/while/body/eval_jaxpr/sba,sbc->sac/dot_general | solution.py:36
  280.7 9.6 %broadcast_multiply_fusion.2 = f32[32,256,256]{2,1,0:T(8,128)} fusion(f32[32]{0:T(128)S(1)} %get-tuple-element.132, bf16[32,256,256]{2,0,1:T(8,128)(2,1)} %copy-done, bf16[32,256,256]{2,1,0:T(8,128)(2,1)} %fusion.71), kind=kOutput, calls=%fused_computation.18.clone.1 | convolution fusion | flops 1075838976 | bytes 16777344 | tf_op jit(solution)/shard_map/while/body/eval_jaxpr/sab,sbc->sac/dot_general | solution.py:39
  290.2 18.8 %scatter_fusion = f32[96,256,256]{2,1,0:T(8,128)} fusion(f32[96,256,256]{2,1,0:T(8,128)} %get-tuple-element.144, s32[32]{0:T(128)S(1)} %fusion.66, f32[32,256,256]{2,1,0:T(8,128)} %broadcast_multiply_fusion.2), kind=kCustom, calls=%fused_computation.1.clone.1 | custom fusion | flops 2097152 | bytes 25165952 | tf_op jit(solution)/shard_map/while/body/eval_jaxpr/scatter-add | solution.py:71
  309.1 7.3 %gather_fusion = bf16[32,256,256]{2,1,0:T(8,128)(2,1)} fusion(bf16[96,256,256]{2,1,0:T(8,128)(2,1)} %get-tuple-element.158, s32[1024]{0:T(1024)S(1)} %pad_clamp_fusion.2), kind=kCustom, calls=%fused_computation.clone.1 | custom fusion | bytes 8388736 | tf_op jit(solution)/shard_map/while/body/eval_jaxpr/jit(_take)/gather | solution.py:69
  318.7 5.0 fusion.70
  323.6 3.3 fusion.69
  327.0 7.5 %copy.28 = bf16[32,256,256]{1,2,0:T(8,128)(2,1)} copy(bf16[32,256,256]{2,0,1:T(8,128)(2,1)} %fusion.69) | data formatting | bytes 8388608 | tf_op jit(solution)/shard_map/while/body/eval_jaxpr/convert_element_type | solution.py:19
  334.5 10.6 %fusion.71 = bf16[32,256,256]{2,1,0:T(8,128)(2,1)} fusion(bf16[32,256,256]{1,2,0:T(8,128)(2,1)} %copy.28, bf16[4,32,256,256]{3,2,1,0:T(8,128)(2,1)} %get-tuple-element.159, s32[]{:T(128)S(6)} %copy.32, f32[32]{0:T(128)S(1)} %get-tuple-element.133, f32[32]{0:T(128)S(1)} %get-tuple-element.132, bf16[32,256,256]{2,1,0:T(8,128)(2,1)} %fusion.70), kind=kOutput, calls=%fused_computation.8.clone.1 | convolution fusion | flops 2157969408 | bytes 20971780 | tf_op jit(solution)/shard_map/while/body/eval_jaxpr/sba,sbc->sac/dot_general | solution.py:36
  345.1 9.6 %broadcast_multiply_fusion.2 = f32[32,256,256]{2,1,0:T(8,128)} fusion(f32[32]{0:T(128)S(1)} %get-tuple-element.132, bf16[32,256,256]{2,0,1:T(8,128)(2,1)} %copy-done, bf16[32,256,256]{2,1,0:T(8,128)(2,1)} %fusion.71), kind=kOutput, calls=%fused_computation.18.clone.1 | convolution fusion | flops 1075838976 | bytes 16777344 | tf_op jit(solution)/shard_map/while/body/eval_jaxpr/sab,sbc->sac/dot_general | solution.py:39
  354.7 18.8 %scatter_fusion = f32[96,256,256]{2,1,0:T(8,128)} fusion(f32[96,256,256]{2,1,0:T(8,128)} %get-tuple-element.144, s32[32]{0:T(128)S(1)} %fusion.66, f32[32,256,256]{2,1,0:T(8,128)} %broadcast_multiply_fusion.2), kind=kCustom, calls=%fused_computation.1.clone.1 | custom fusion | flops 2097152 | bytes 25165952 | tf_op jit(solution)/shard_map/while/body/eval_jaxpr/scatter-add | solution.py:71
  373.5 13.2 %convert_element_type.64 = bf16[96,256,256]{2,1,0:T(8,128)(2,1)} convert(f32[96,256,256]{2,1,0:T(8,128)} %get-tuple-element.44) | non-fusion elementwise | flops 6291456 | bytes 37748736 | tf_op jit(solution)/shard_map/convert_element_type | solution.py:77
  386.7 94.3 %reduce-scatter.4.cloned.1.call-done = bf16[1,1,6,256,256]{4,3,2,1,0:T(8,128)(2,1)} async-done(((bf16[16,1,6,256,256]{4,3,2,1,0:T(8,128)(2,1)}), bf16[1,1,6,256,256]{4,3,2,1,0:T(8,128)(2,1)}) %reduce-scatter.4.cloned.1.call-update) | async-done | bytes 786448
  484.2 64.5 %psum.7 = f32[]{:T(128)} all-reduce(f32[]{:T(128)} %get-tuple-element.79), channel_id=1, replica_groups=mesh['patch'=16,'exp'=8] {'patch','exp'}, use_global_device_ids=true, to_apply=%region_5.6 | all-reduce | flops 1 | bytes 8 | tf_op jit(solution)/shard_map/psum | solution.py:84
  (60 shorter events, 24.4 us)
Async XLA Ops:
  7.2 96.9 %all-gather.2.cloned.1.call-start = ((), (), s32[]{:S(2)}) async-start(), calls=%async_computation.1 | async-start | bytes 13369344 | tf_op jit(solution)/shard_map/all_gather | solution.py:54
  9.6 471.4 %reduce-scatter.4.cloned.1.call-start = ((), (), s32[]{:S(2)}) async-start(), calls=%async_computation.2 | async-start | bytes 13369344
  123.0 2.2 copy-start.1
  125.2 5.0 copy-start
  187.5 2.2 copy-start.1
  189.7 5.0 copy-start
  252.0 2.2 copy-start.1
  254.2 5.0 copy-start
  316.5 2.2 copy-start.1
  318.7 5.0 copy-start
  386.7 94.3 %copy-start.2 = (f32[1,1,6,256,256]{4,3,2,1,0:T(8,128)S(1)}, f32[1,1,6,256,256]{4,3,2,1,0:T(8,128)}, u32[]{:S(2)}) copy-start(f32[1,1,6,256,256]{4,3,2,1,0:T(8,128)} %param.9) | copy-start | bytes 4718596
Sparse Core Ops, SparseCore 0:
  10.7 93.3 all-gather.1
  386.8 94.1 reduce-scatter.3
where the time goes:
time: 559 us; the launch traced here: 557 us
  waiting for transfers between devices  186 us (33%)
  matrix products  119 us (21%)
  other arithmetic  94.9 us (17%)
  local copies, waits for them, and re-layouts  77 us (14%)
  blocking collectives  64.5 us (12%)
  between operations  15.9 us (3%)
    unnamed x3, waiting for transfers between devices  94.3 us
    all_gather x1, waiting for transfers between devices, per_device(): gathered = lax.all_gather(model_half, 'patch', axis=0, tiled=True)  91.4 us
    scatter-add x4, other arithmetic, source_block(): return (running.at[keys_block].add(adjoint), None)  75.2 us
    psum x1, blocking collectives, per_device(): square_sum = lax.psum(jnp.sum(step_field * step_field), ('patch', 'exp'))  64.5 us
    dot_general x4, matrix products, stamp_adjoint(): jnp.einsum('sba,sbc->sac', row_kernel, residual, preferred_element_type=j...  42.6 us
    dot_general x4, matrix products, stamp_adjoint(): jnp.einsum('sab,sbc->sac', backward, col_kernel, preferred_element_type=j...  38.3 us
    convert_element_type x4, local copies, waits for them, and re-layouts, banded_matrices(): return jnp.einsum('sk,kij->sij', tap_values, tap_table, preferred_element...  30.1 us
    gather x4, local copies, waits for them, and re-layouts, source_block(): tile_sel = jnp.take(flat_tiles, keys_block, axis=0)  29.4 us
  transfers between devices with their start and end apart: 2, of which 2 were waited for; matrix products, arithmetic and copies ran while one was open for 1% of the time, Pallas kernels for 0%

commit v1 on v0

--- a/solution.py
+++ b/solution.py
@@ -51,7 +51,25 @@
     block_rows = 32
     model_half = sky_model.astype(jnp.bfloat16)
     patches = lax.axis_size("patch")
-    gathered = lax.all_gather(model_half, "patch", axis=0, tiled=True)
+    count, index, width = (lax.axis_size("patch"), lax.axis_index("patch"), model_half.shape[0])
+    right = [(i, (i + 1) % count) for i in range(count)]
+    downward = [(i, (i - 1) % count) for i in range(count)]
+    gathered = jnp.zeros(
+        (*model_half.shape[:0], count * width, *model_half.shape[0 + 1 :]), model_half.dtype
+    )
+    gathered = lax.dynamic_update_slice_in_dim(gathered, model_half, index * width, axis=0)
+    from_left = from_right = model_half
+    half = count // 2
+    for step in range(1, half + 1):
+        from_left = lax.ppermute(from_left, "patch", right)
+        gathered = lax.dynamic_update_slice_in_dim(
+            gathered, from_left, (index - step) % count * width, axis=0
+        )
+        if step < count - half:
+            from_right = lax.ppermute(from_right, "patch", downward)
+            gathered = lax.dynamic_update_slice_in_dim(
+                gathered, from_right, (index + step) % count * width, axis=0
+            )
     key_count = gathered.shape[0] * band_count
     flat_tiles = gathered.reshape(key_count, tile_size, tile_size)
     tile_keys = stamp_patch[:, 0] * band_count + stamp_band

time: 559 us -> 640 us (1.14)
  starting transfers between devices: 0.08 us -> 36.4 us
  local copies, waits for them, and re-layouts: 77 us -> 103 us
  waiting for transfers between devices: 186 us -> 197 us
  matrix products: 119 us -> 129 us
    ppermute x0 -> x15, waiting for transfers between devices: none -> 99.1 us  [the longest x8 99 us: per_device(): from_left = lax.ppermute(from_left, 'patch', right)]
    all_gather x1 -> x0, waiting for transfers between devices: 91.4 us -> none  [per_device(): gathered = lax.all_gather(model_half, 'patch', axis=0, tiled=True)]
    ppermute x0 -> x15, starting transfers between devices: none -> 36.4 us  [the longest x7 34.4 us: per_device(): from_right = lax.ppermute(from_right, 'patch', downward)]
    dynamic_update_slice x0 -> x15, local copies, waits for them, and re-layouts: none -> 17.7 us  [the longest x7 8.88 us: per_device(): lax.dynamic_update_slice_in_dim(gathered, from_right, (index + step) % co...]
    dot_general x4, matrix products: 19.8 us -> 29.1 us  [stamp_adjoint(): jnp.einsum('sab,scb->sac', tile_sel, col_kernel, preferred_element_type=j...]
    unnamed x3 -> x2, waiting for transfers between devices: 94.3 us -> 97.9 us
  transfers between devices with their start and end apart: 2 -> 16, of which waited for: 2 -> 10; matrix products, arithmetic and copies ran while one was open for 1% -> 3% of each run, Pallas kernels for 0% -> 0%
where the time goes in v1:
time: 640 us; the launch traced here: 639 us
  waiting for transfers between devices  197 us (31%)
  matrix products  129 us (20%)
  local copies, waits for them, and re-layouts  103 us (16%)
  other arithmetic  92.8 us (14%)
  blocking collectives  64.5 us (10%)
  starting transfers between devices  36.4 us (6%)
  between operations  16.3 us (3%)
    ppermute x8, waiting for transfers between devices, per_device(): from_left = lax.ppermute(from_left, 'patch', right)  99 us
    unnamed x2, waiting for transfers between devices  97.9 us
    scatter-add x4, other arithmetic, source_block(): return (running.at[keys_block].add(adjoint), None)  75.1 us
    psum x1, blocking collectives, per_device(): square_sum = lax.psum(jnp.sum(step_field * step_field), ('patch', 'exp'))  64.5 us
    dot_general x4, matrix products, stamp_adjoint(): jnp.einsum('sba,sbc->sac', row_kernel, residual, preferred_element_type=j...  42.7 us
    dot_general x4, matrix products, stamp_adjoint(): jnp.einsum('sab,sbc->sac', backward, col_kernel, preferred_element_type=j...  38.2 us
    ppermute x7, starting transfers between devices, per_device(): from_right = lax.ppermute(from_right, 'patch', downward)  34.4 us
    convert_element_type x4, local copies, waits for them, and re-layouts, banded_matrices(): return jnp.einsum('sk,kij->sij', tap_values, tap_table, preferred_element...  30.1 us
  transfers between devices with their start and end apart: 16, of which 10 were waited for; matrix products, arithmetic and copies ran while one was open for 3% of the time, Pallas kernels for 0%

profile of v1, /device:TPU:1, one launch (start us, length us, event | category | flops | bytes accessed | tf_op | source)
XLA Modules:
  0.0 638.5 jit_solution(4541590642013156706)
XLA Ops:
  21.2 17.3 %collective-permute-done = bf16[1,1,6,256,256]{4,3,2,1,0:T(8,128)(2,1)S(1)} collective-permute-done((bf16[1,1,6,256,256]{4,3,2,1,0:T(8,128)(2,1)S(1)}, bf16[1,1,6,256,256]{4,3,2,1,0:T(8,128)(2,1)S(1)}, u32[]{:S(2)}, u32[]{:S(2)}) %collective-permute-start) | collective-permute-done | bytes 786464 | tf_op jit(solution)/shard_map/ppermute | solution.py:64
  43.3 16.3 %collective-permute-done.2 = bf16[1,1,6,256,256]{4,3,2,1,0:T(8,128)(2,1)S(1)} collective-permute-done((bf16[1,1,6,256,256]{4,3,2,1,0:T(8,128)(2,1)S(1)}, bf16[1,1,6,256,256]{4,3,2,1,0:T(8,128)(2,1)S(1)}, u32[]{:S(2)}, u32[]{:S(2)}) %collective-permute-start.2) | collective-permute-done | bytes 786464 | tf_op jit(solution)/shard_map/ppermute | solution.py:64
  64.4 15.4 %collective-permute-done.4 = bf16[1,1,6,256,256]{4,3,2,1,0:T(8,128)(2,1)S(1)} collective-permute-done((bf16[1,1,6,256,256]{4,3,2,1,0:T(8,128)(2,1)S(1)}, bf16[1,1,6,256,256]{4,3,2,1,0:T(8,128)(2,1)S(1)}, u32[]{:S(2)}, u32[]{:S(2)}) %collective-permute-start.4) | collective-permute-done | bytes 786464 | tf_op jit(solution)/shard_map/ppermute | solution.py:64
  89.2 9.9 %collective-permute-done.6 = bf16[1,1,6,256,256]{4,3,2,1,0:T(8,128)(2,1)S(1)} collective-permute-done((bf16[1,1,6,256,256]{4,3,2,1,0:T(8,128)(2,1)S(1)}, bf16[1,1,6,256,256]{4,3,2,1,0:T(8,128)(2,1)S(1)}, u32[]{:S(2)}, u32[]{:S(2)}) %collective-permute-start.6) | collective-permute-done | bytes 786464 | tf_op jit(solution)/shard_map/ppermute | solution.py:64
  107.8 9.6 %collective-permute-done.8 = bf16[1,1,6,256,256]{4,3,2,1,0:T(8,128)(2,1)S(1)} collective-permute-done((bf16[1,1,6,256,256]{4,3,2,1,0:T(8,128)(2,1)S(1)}, bf16[1,1,6,256,256]{4,3,2,1,0:T(8,128)(2,1)S(1)}, u32[]{:S(2)}, u32[]{:S(2)}) %collective-permute-start.8) | collective-permute-done | bytes 786464 | tf_op jit(solution)/shard_map/ppermute | solution.py:64
  125.9 9.0 %collective-permute-done.10 = bf16[1,1,6,256,256]{4,3,2,1,0:T(8,128)(2,1)S(1)} collective-permute-done((bf16[1,1,6,256,256]{4,3,2,1,0:T(8,128)(2,1)S(1)}, bf16[1,1,6,256,256]{4,3,2,1,0:T(8,128)(2,1)S(1)}, u32[]{:S(2)}, u32[]{:S(2)}) %collective-permute-start.10) | collective-permute-done | bytes 786464 | tf_op jit(solution)/shard_map/ppermute | solution.py:64
  143.1 8.3 %collective-permute-done.12 = bf16[1,1,6,256,256]{4,3,2,1,0:T(8,128)(2,1)S(1)} collective-permute-done((bf16[1,1,6,256,256]{4,3,2,1,0:T(8,128)(2,1)S(1)}, bf16[1,1,6,256,256]{4,3,2,1,0:T(8,128)(2,1)S(1)}, u32[]{:S(2)}, u32[]{:S(2)}) %collective-permute-start.12) | collective-permute-done | bytes 786464 | tf_op jit(solution)/shard_map/ppermute | solution.py:64
  154.3 13.2 %collective-permute-done.14 = bf16[1,1,6,256,256]{4,3,2,1,0:T(8,128)(2,1)S(1)} collective-permute-done((bf16[1,1,6,256,256]{4,3,2,1,0:T(8,128)(2,1)S(1)}, bf16[1,1,6,256,256]{4,3,2,1,0:T(8,128)(2,1)S(1)}, u32[]{:S(2)}, u32[]{:S(2)}) %collective-permute-start.14) | collective-permute-done | bytes 786464 | tf_op jit(solution)/shard_map/ppermute | solution.py:64
  168.4 11.4 %broadcast_in_dim.14 = f32[96,256,256]{2,1,0:T(8,128)} broadcast(f32[]{:T(128)} %constant.129.clone.1), dimensions={} | broadcast | bytes 25165828 | tf_op jit(solution)/shard_map/broadcast_in_dim | solution.py:92
  179.8 271.2 %while.10 = (s32[]{:T(128)}, f32[96,256,256]{2,1,0:T(8,128)}, s32[4,32]{1,0:T(4,128)S(1)}, bf16[4,32]{1,0:T(4,128)(2,1)S(1)}, bf16[4,32,2,21]{1,3,2,0:T(8,128)(2...) while((s32[]{:T(128)}, f32[96,256,256]{2,1,0:T(8,128)}, ...), condition=%wide.region_2.3_spmd, body=%wide.region_0.2_spmd.sunk | while | flops 4494984704 | bytes 118250448 | solution.py:91
  179.9 7.3 %gather_fusion = bf16[32,256,256]{2,1,0:T(8,128)(2,1)} fusion(bf16[96,256,256]{2,1,0:T(8,128)(2,1)} %get-tuple-element.160, s32[1024]{0:T(1024)S(1)} %pad_clamp_fusion.2), kind=kCustom, calls=%fused_computation.clone.1 | custom fusion | bytes 8388736 | tf_op jit(solution)/shard_map/while/body/eval_jaxpr/jit(_take)/gather | solution.py:87
  201.1 7.5 %copy.76 = bf16[32,256,256]{1,2,0:T(8,128)(2,1)} copy(bf16[32,256,256]{2,0,1:T(8,128)(2,1)} %fusion.69) | data formatting | bytes 8388608 | tf_op jit(solution)/shard_map/while/body/eval_jaxpr/convert_element_type | solution.py:19
  208.7 10.7 %fusion.71 = bf16[32,256,256]{2,1,0:T(8,128)(2,1)} fusion(bf16[32,256,256]{1,2,0:T(8,128)(2,1)} %copy.76, bf16[4,32,256,256]{3,2,1,0:T(8,128)(2,1)} %get-tuple-element.161, s32[]{:T(128)S(6)} %copy.96, f32[32]{0:T(128)S(1)} %get-tuple-element.135, f32[32]{0:T(128)S(1)} %get-tuple-element.134, bf16[32,256,256]{2,1,0:T(8,128)(2,1)} %fusion.70), kind=kOutput, calls=%fused_computation.8.clone.1 | convolution fusion | flops 2157969408 | bytes 20971780 | tf_op jit(solution)/shard_map/while/body/eval_jaxpr/sba,sbc->sac/dot_general | solution.py:36
  219.3 9.5 %broadcast_multiply_fusion.2 = f32[32,256,256]{2,1,0:T(8,128)} fusion(f32[32]{0:T(128)S(1)} %get-tuple-element.134, bf16[32,256,256]{2,0,1:T(8,128)(2,1)} %copy-done, bf16[32,256,256]{2,1,0:T(8,128)(2,1)} %fusion.71), kind=kOutput, calls=%fused_computation.18.clone.1 | convolution fusion | flops 1075838976 | bytes 16777344 | tf_op jit(solution)/shard_map/while/body/eval_jaxpr/sab,sbc->sac/dot_general | solution.py:39
  228.9 18.7 %scatter_fusion = f32[96,256,256]{2,1,0:T(8,128)} fusion(f32[96,256,256]{2,1,0:T(8,128)} %get-tuple-element.146, s32[32]{0:T(128)S(1)} %fusion.66, f32[32,256,256]{2,1,0:T(8,128)} %broadcast_multiply_fusion.2), kind=kCustom, calls=%fused_computation.1.clone.1 | custom fusion | flops 2097152 | bytes 25165952 | tf_op jit(solution)/shard_map/while/body/eval_jaxpr/scatter-add | solution.py:89
  247.7 7.3 %gather_fusion = bf16[32,256,256]{2,1,0:T(8,128)(2,1)} fusion(bf16[96,256,256]{2,1,0:T(8,128)(2,1)} %get-tuple-element.160, s32[1024]{0:T(1024)S(1)} %pad_clamp_fusion.2), kind=kCustom, calls=%fused_computation.clone.1 | custom fusion | bytes 8388736 | tf_op jit(solution)/shard_map/while/body/eval_jaxpr/jit(_take)/gather | solution.py:87
  268.9 7.5 %copy.76 = bf16[32,256,256]{1,2,0:T(8,128)(2,1)} copy(bf16[32,256,256]{2,0,1:T(8,128)(2,1)} %fusion.69) | data formatting | bytes 8388608 | tf_op jit(solution)/shard_map/while/body/eval_jaxpr/convert_element_type | solution.py:19
  276.4 10.7 %fusion.71 = bf16[32,256,256]{2,1,0:T(8,128)(2,1)} fusion(bf16[32,256,256]{1,2,0:T(8,128)(2,1)} %copy.76, bf16[4,32,256,256]{3,2,1,0:T(8,128)(2,1)} %get-tuple-element.161, s32[]{:T(128)S(6)} %copy.96, f32[32]{0:T(128)S(1)} %get-tuple-element.135, f32[32]{0:T(128)S(1)} %get-tuple-element.134, bf16[32,256,256]{2,1,0:T(8,128)(2,1)} %fusion.70), kind=kOutput, calls=%fused_computation.8.clone.1 | convolution fusion | flops 2157969408 | bytes 20971780 | tf_op jit(solution)/shard_map/while/body/eval_jaxpr/sba,sbc->sac/dot_general | solution.py:36
  287.1 9.5 %broadcast_multiply_fusion.2 = f32[32,256,256]{2,1,0:T(8,128)} fusion(f32[32]{0:T(128)S(1)} %get-tuple-element.134, bf16[32,256,256]{2,0,1:T(8,128)(2,1)} %copy-done, bf16[32,256,256]{2,1,0:T(8,128)(2,1)} %fusion.71), kind=kOutput, calls=%fused_computation.18.clone.1 | convolution fusion | flops 1075838976 | bytes 16777344 | tf_op jit(solution)/shard_map/while/body/eval_jaxpr/sab,sbc->sac/dot_general | solution.py:39
  296.6 18.7 %scatter_fusion = f32[96,256,256]{2,1,0:T(8,128)} fusion(f32[96,256,256]{2,1,0:T(8,128)} %get-tuple-element.146, s32[32]{0:T(128)S(1)} %fusion.66, f32[32,256,256]{2,1,0:T(8,128)} %broadcast_multiply_fusion.2), kind=kCustom, calls=%fused_computation.1.clone.1 | custom fusion | flops 2097152 | bytes 25165952 | tf_op jit(solution)/shard_map/while/body/eval_jaxpr/scatter-add | solution.py:89
  315.4 7.3 %gather_fusion = bf16[32,256,256]{2,1,0:T(8,128)(2,1)} fusion(bf16[96,256,256]{2,1,0:T(8,128)(2,1)} %get-tuple-element.160, s32[1024]{0:T(1024)S(1)} %pad_clamp_fusion.2), kind=kCustom, calls=%fused_computation.clone.1 | custom fusion | bytes 8388736 | tf_op jit(solution)/shard_map/while/body/eval_jaxpr/jit(_take)/gather | solution.py:87
  336.6 7.5 %copy.76 = bf16[32,256,256]{1,2,0:T(8,128)(2,1)} copy(bf16[32,256,256]{2,0,1:T(8,128)(2,1)} %fusion.69) | data formatting | bytes 8388608 | tf_op jit(solution)/shard_map/while/body/eval_jaxpr/convert_element_type | solution.py:19
  344.2 10.7 %fusion.71 = bf16[32,256,256]{2,1,0:T(8,128)(2,1)} fusion(bf16[32,256,256]{1,2,0:T(8,128)(2,1)} %copy.76, bf16[4,32,256,256]{3,2,1,0:T(8,128)(2,1)} %get-tuple-element.161, s32[]{:T(128)S(6)} %copy.96, f32[32]{0:T(128)S(1)} %get-tuple-element.135, f32[32]{0:T(128)S(1)} %get-tuple-element.134, bf16[32,256,256]{2,1,0:T(8,128)(2,1)} %fusion.70), kind=kOutput, calls=%fused_computation.8.clone.1 | convolution fusion | flops 2157969408 | bytes 20971780 | tf_op jit(solution)/shard_map/while/body/eval_jaxpr/sba,sbc->sac/dot_general | solution.py:36
  354.8 9.5 %broadcast_multiply_fusion.2 = f32[32,256,256]{2,1,0:T(8,128)} fusion(f32[32]{0:T(128)S(1)} %get-tuple-element.134, bf16[32,256,256]{2,0,1:T(8,128)(2,1)} %copy-done, bf16[32,256,256]{2,1,0:T(8,128)(2,1)} %fusion.71), kind=kOutput, calls=%fused_computation.18.clone.1 | convolution fusion | flops 1075838976 | bytes 16777344 | tf_op jit(solution)/shard_map/while/body/eval_jaxpr/sab,sbc->sac/dot_general | solution.py:39
  364.4 18.8 %scatter_fusion = f32[96,256,256]{2,1,0:T(8,128)} fusion(f32[96,256,256]{2,1,0:T(8,128)} %get-tuple-element.146, s32[32]{0:T(128)S(1)} %fusion.66, f32[32,256,256]{2,1,0:T(8,128)} %broadcast_multiply_fusion.2), kind=kCustom, calls=%fused_computation.1.clone.1 | custom fusion | flops 2097152 | bytes 25165952 | tf_op jit(solution)/shard_map/while/body/eval_jaxpr/scatter-add | solution.py:89
  404.5 7.5 %copy.76 = bf16[32,256,256]{1,2,0:T(8,128)(2,1)} copy(bf16[32,256,256]{2,0,1:T(8,128)(2,1)} %fusion.69) | data formatting | bytes 8388608 | tf_op jit(solution)/shard_map/while/body/eval_jaxpr/convert_element_type | solution.py:19
  412.1 10.7 %fusion.71 = bf16[32,256,256]{2,1,0:T(8,128)(2,1)} fusion(bf16[32,256,256]{1,2,0:T(8,128)(2,1)} %copy.76, bf16[4,32,256,256]{3,2,1,0:T(8,128)(2,1)} %get-tuple-element.161, s32[]{:T(128)S(6)} %copy.96, f32[32]{0:T(128)S(1)} %get-tuple-element.135, f32[32]{0:T(128)S(1)} %get-tuple-element.134, bf16[32,256,256]{2,1,0:T(8,128)(2,1)} %fusion.70), kind=kOutput, calls=%fused_computation.8.clone.1 | convolution fusion | flops 2157969408 | bytes 20971780 | tf_op jit(solution)/shard_map/while/body/eval_jaxpr/sba,sbc->sac/dot_general | solution.py:36
  422.7 9.5 %broadcast_multiply_fusion.2 = f32[32,256,256]{2,1,0:T(8,128)} fusion(f32[32]{0:T(128)S(1)} %get-tuple-element.134, bf16[32,256,256]{2,0,1:T(8,128)(2,1)} %copy-done, bf16[32,256,256]{2,1,0:T(8,128)(2,1)} %fusion.71), kind=kOutput, calls=%fused_computation.18.clone.1 | convolution fusion | flops 1075838976 | bytes 16777344 | tf_op jit(solution)/shard_map/while/body/eval_jaxpr/sab,sbc->sac/dot_general | solution.py:39
  432.3 18.8 %scatter_fusion = f32[96,256,256]{2,1,0:T(8,128)} fusion(f32[96,256,256]{2,1,0:T(8,128)} %get-tuple-element.146, s32[32]{0:T(128)S(1)} %fusion.66, f32[32,256,256]{2,1,0:T(8,128)} %broadcast_multiply_fusion.2), kind=kCustom, calls=%fused_computation.1.clone.1 | custom fusion | flops 2097152 | bytes 25165952 | tf_op jit(solution)/shard_map/while/body/eval_jaxpr/scatter-add | solution.py:89
  451.1 13.2 %convert_element_type.64 = bf16[96,256,256]{2,1,0:T(8,128)(2,1)} convert(f32[96,256,256]{2,1,0:T(8,128)} %get-tuple-element.44) | non-fusion elementwise | flops 6291456 | bytes 37748736 | tf_op jit(solution)/shard_map/convert_element_type | solution.py:95
  464.3 97.9 %reduce-scatter.4.cloned.1.call-done = bf16[1,1,6,256,256]{4,3,2,1,0:T(8,128)(2,1)} async-done(((bf16[16,1,6,256,256]{4,3,2,1,0:T(8,128)(2,1)}), bf16[1,1,6,256,256]{4,3,2,1,0:T(8,128)(2,1)}) %reduce-scatter.4.cloned.1.call-update) | async-done | bytes 786448
  565.4 64.5 %psum.7 = f32[]{:T(128)} all-reduce(f32[]{:T(128)} %get-tuple-element.81), channel_id=1, replica_groups=mesh['patch'=16,'exp'=8] {'patch','exp'}, use_global_device_ids=true, to_apply=%region_5.6 | all-reduce | flops 1 | bytes 8 | tf_op jit(solution)/shard_map/psum | solution.py:102
  (111 shorter events, 128.0 us)
Async XLA Ops:
  7.2 6.3 copy-start.1
  7.2 72.9 %copy-start.6 = (bf16[128]{0:T(256)(128)(2,1)S(1)}, bf16[128]{0:T(256)(128)(2,1)}, u32[]{:S(2)}) copy-start(bf16[128]{0:T(256)(128)(2,1)} %param.14) | copy-start | bytes 772
  7.2 73.0 %copy-start.7 = (bf16[128]{0:T(256)(128)(2,1)S(1)}, bf16[128]{0:T(256)(128)(2,1)}, u32[]{:S(2)}) copy-start(bf16[128]{0:T(256)(128)(2,1)} %param.15) | copy-start | bytes 772
  7.2 73.1 %copy-start.8 = (s32[128]{0:T(128)S(1)}, s32[128]{0:T(128)}, u32[]{:S(2)}) copy-start(s32[128]{0:T(128)} %param.12) | copy-start | bytes 1540
  7.2 73.1 %copy-start.9 = (s32[128,1]{0,1:T(1,128)S(1)}, s32[128,1]{0,1:T(1,128)}, u32[]{:S(2)}) copy-start(s32[128,1]{0,1:T(1,128)} %param.11) | copy-start | bytes 1540
  7.2 73.2 %copy-start.5 = (bf16[128,2,21]{0,1,2:T(2,128)(2,1)S(1)}, bf16[128,2,21]{0,1,2:T(2,128)(2,1)}, u32[]{:S(2)}) copy-start(bf16[128,2,21]{0,1,2:T(2,128)(2,1)} %param.13) | copy-start | bytes 32260
  7.2 554.9 %reduce-scatter.4.cloned.1.call-start = ((), (), s32[]{:S(2)}) async-start(), calls=%async_computation.1 | async-start | bytes 13369344
  14.5 24.0 %collective-permute-start = (bf16[1,1,6,256,256]{4,3,2,1,0:T(8,128)(2,1)S(1)}, bf16[1,1,6,256,256]{4,3,2,1,0:T(8,128)(2,1)S(1)}, u32[]{:S(2)}, u32[]{:S(2)}) collective-permute-start(bf16[1,1,6,256,256]{4,3,2,1,0:T(8,128)(2,1)S(1)} %get-tuple-element.78), channel_id=1, source_target_pairs={{0,8},{8,16},{16,24},{24,32},{32,40},{40,48},{48,56},{56,64},{64,7... | collective-permute-start | bytes 2359304 | tf_op jit(solution)/shard_map/ppermute | solution.py:64
  16.5 22.0 %collective-permute-start.1 = (bf16[1,1,6,256,256]{4,3,2,1,0:T(8,128)(2,1)S(1)}, bf16[1,1,6,256,256]{4,3,2,1,0:T(8,128)(2,1)S(1)}, u32[]{:S(2)}, u32[]{:S(2)}) collective-permute-start(bf16[1,1,6,256,256]{4,3,2,1,0:T(8,128)(2,1)S(1)} %get-tuple-element.78), channel_id=1, source_target_pairs={{0,120},{8,0},{16,8},{24,16},{32,24},{40,32},{48,40},{56,48},{64,5... | collective-permute-start | bytes 2359304 | tf_op jit(solution)/shard_map/ppermute | solution.py:69
  38.5 41.3 %copy-start.4 = (bf16[1,1,6,256,256]{4,3,2,1,0:T(8,128)(2,1)}, bf16[1,1,6,256,256]{4,3,2,1,0:T(8,128)(2,1)S(1)}, u32[]{:S(2)}) copy-start(bf16[1,1,6,256,256]{4,3,2,1,0:T(8,128)(2,1)S(1)} %collective-permute-done) | copy-start | bytes 2359300
  38.5 21.1 %collective-permute-start.2 = (bf16[1,1,6,256,256]{4,3,2,1,0:T(8,128)(2,1)S(1)}, bf16[1,1,6,256,256]{4,3,2,1,0:T(8,128)(2,1)S(1)}, u32[]{:S(2)}, u32[]{:S(2)}) collective-permute-start(bf16[1,1,6,256,256]{4,3,2,1,0:T(8,128)(2,1)S(1)} %collective-permute-done), channel_id=1, source_target_pairs={{0,8},{8,16},{16,24},{24,32},{32,40},{40,48},{48,56},{56,64},{64,7... | collective-permute-start | bytes 2359304 | tf_op jit(solution)/shard_map/ppermute | solution.py:64
  38.5 41.3 %copy-start.3 = (bf16[1,1,6,256,256]{4,3,2,1,0:T(8,128)(2,1)}, bf16[1,1,6,256,256]{4,3,2,1,0:T(8,128)(2,1)S(1)}, u32[]{:S(2)}) copy-start(bf16[1,1,6,256,256]{4,3,2,1,0:T(8,128)(2,1)S(1)} %collective-permute-done.1) | copy-start | bytes 2359300
  38.5 21.1 %collective-permute-start.3 = (bf16[1,1,6,256,256]{4,3,2,1,0:T(8,128)(2,1)S(1)}, bf16[1,1,6,256,256]{4,3,2,1,0:T(8,128)(2,1)}, u32[]{:S(2)}, u32[]{:S(2)}) collective-permute-start(bf16[1,1,6,256,256]{4,3,2,1,0:T(8,128)(2,1)S(1)} %collective-permute-done.1), channel_id=1, source_target_pairs={{0,120},{8,0},{16,8},{24,16},{32,24},{40,32},{48,40},{56,48},{64,5... | collective-permute-start | bytes 2359304 | tf_op jit(solution)/shard_map/ppermute | solution.py:69
  59.6 20.2 %collective-permute-start.4 = (bf16[1,1,6,256,256]{4,3,2,1,0:T(8,128)(2,1)S(1)}, bf16[1,1,6,256,256]{4,3,2,1,0:T(8,128)(2,1)S(1)}, u32[]{:S(2)}, u32[]{:S(2)}) collective-permute-start(bf16[1,1,6,256,256]{4,3,2,1,0:T(8,128)(2,1)S(1)} %collective-permute-done.2), channel_id=1, source_target_pairs={{0,8},{8,16},{16,24},{24,32},{32,40},{40,48},{48,56},{56,64},{64,7... | collective-permute-start | bytes 2359304 | tf_op jit(solution)/shard_map/ppermute | solution.py:64
  59.6 23.0 %collective-permute-start.5 = (bf16[1,1,6,256,256]{4,3,2,1,0:T(8,128)(2,1)}, bf16[1,1,6,256,256]{4,3,2,1,0:T(8,128)(2,1)S(1)}, u32[]{:S(2)}, u32[]{:S(2)}) collective-permute-start(bf16[1,1,6,256,256]{4,3,2,1,0:T(8,128)(2,1)} %collective-permute-done.3), channel_id=1, source_target_pairs={{0,120},{8,0},{16,8},{24,16},{32,24},{40,32},{48,40},{56,48},{64,5... | collective-permute-start | bytes 2359304 | tf_op jit(solution)/shard_map/ppermute | solution.py:69
  79.8 19.3 %collective-permute-start.6 = (bf16[1,1,6,256,256]{4,3,2,1,0:T(8,128)(2,1)S(1)}, bf16[1,1,6,256,256]{4,3,2,1,0:T(8,128)(2,1)S(1)}, u32[]{:S(2)}, u32[]{:S(2)}) collective-permute-start(bf16[1,1,6,256,256]{4,3,2,1,0:T(8,128)(2,1)S(1)} %collective-permute-done.4), channel_id=1, source_target_pairs={{0,8},{8,16},{16,24},{24,32},{32,40},{40,48},{48,56},{56,64},{64,7... | collective-permute-start | bytes 2359304 | tf_op jit(solution)/shard_map/ppermute | solution.py:64
  82.7 19.5 %collective-permute-start.7 = (bf16[1,1,6,256,256]{4,3,2,1,0:T(8,128)(2,1)S(1)}, bf16[1,1,6,256,256]{4,3,2,1,0:T(8,128)(2,1)S(1)}, u32[]{:S(2)}, u32[]{:S(2)}) collective-permute-start(bf16[1,1,6,256,256]{4,3,2,1,0:T(8,128)(2,1)S(1)} %collective-permute-done.5), channel_id=1, source_target_pairs={{0,120},{8,0},{16,8},{24,16},{32,24},{40,32},{48,40},{56,48},{64,5... | collective-permute-start | bytes 2359304 | tf_op jit(solution)/shard_map/ppermute | solution.py:69
  99.1 18.4 %collective-permute-start.8 = (bf16[1,1,6,256,256]{4,3,2,1,0:T(8,128)(2,1)S(1)}, bf16[1,1,6,256,256]{4,3,2,1,0:T(8,128)(2,1)S(1)}, u32[]{:S(2)}, u32[]{:S(2)}) collective-permute-start(bf16[1,1,6,256,256]{4,3,2,1,0:T(8,128)(2,1)S(1)} %collective-permute-done.6), channel_id=1, source_target_pairs={{0,8},{8,16},{16,24},{24,32},{32,40},{40,48},{48,56},{56,64},{64,7... | collective-permute-start | bytes 2359304 | tf_op jit(solution)/shard_map/ppermute | solution.py:64
  102.1 17.3 %collective-permute-start.9 = (bf16[1,1,6,256,256]{4,3,2,1,0:T(8,128)(2,1)S(1)}, bf16[1,1,6,256,256]{4,3,2,1,0:T(8,128)(2,1)S(1)}, u32[]{:S(2)}, u32[]{:S(2)}) collective-permute-start(bf16[1,1,6,256,256]{4,3,2,1,0:T(8,128)(2,1)S(1)} %collective-permute-done.7), channel_id=1, source_target_pairs={{0,120},{8,0},{16,8},{24,16},{32,24},{40,32},{48,40},{56,48},{64,5... | collective-permute-start | bytes 2359304 | tf_op jit(solution)/shard_map/ppermute | solution.py:69
  117.5 17.4 %collective-permute-start.10 = (bf16[1,1,6,256,256]{4,3,2,1,0:T(8,128)(2,1)S(1)}, bf16[1,1,6,256,256]{4,3,2,1,0:T(8,128)(2,1)S(1)}, u32[]{:S(2)}, u32[]{:S(2)}) collective-permute-start(bf16[1,1,6,256,256]{4,3,2,1,0:T(8,128)(2,1)S(1)} %collective-permute-done.8), channel_id=1, source_target_pairs={{0,8},{8,16},{16,24},{24,32},{32,40},{40,48},{48,56},{56,64},{64,7... | collective-permute-start | bytes 2359304 | tf_op jit(solution)/shard_map/ppermute | solution.py:64
  119.5 17.4 %collective-permute-start.11 = (bf16[1,1,6,256,256]{4,3,2,1,0:T(8,128)(2,1)S(1)}, bf16[1,1,6,256,256]{4,3,2,1,0:T(8,128)(2,1)S(1)}, u32[]{:S(2)}, u32[]{:S(2)}) collective-permute-start(bf16[1,1,6,256,256]{4,3,2,1,0:T(8,128)(2,1)S(1)} %collective-permute-done.9), channel_id=1, source_target_pairs={{0,120},{8,0},{16,8},{24,16},{32,24},{40,32},{48,40},{56,48},{64,5... | collective-permute-start | bytes 2359304 | tf_op jit(solution)/shard_map/ppermute | solution.py:69
  134.9 16.5 %collective-permute-start.12 = (bf16[1,1,6,256,256]{4,3,2,1,0:T(8,128)(2,1)S(1)}, bf16[1,1,6,256,256]{4,3,2,1,0:T(8,128)(2,1)S(1)}, u32[]{:S(2)}, u32[]{:S(2)}) collective-permute-start(bf16[1,1,6,256,256]{4,3,2,1,0:T(8,128)(2,1)S(1)} %collective-permute-done.10), channel_id=1, source_target_pairs={{0,8},{8,16},{16,24},{24,32},{32,40},{40,48},{48,56},{56,64},{64,7... | collective-permute-start | bytes 2359304 | tf_op jit(solution)/shard_map/ppermute | solution.py:64
  136.9 16.4 %collective-permute-start.13 = (bf16[1,1,6,256,256]{4,3,2,1,0:T(8,128)(2,1)S(1)}, bf16[1,1,6,256,256]{4,3,2,1,0:T(8,128)(2,1)S(1)}, u32[]{:S(2)}, u32[]{:S(2)}) collective-permute-start(bf16[1,1,6,256,256]{4,3,2,1,0:T(8,128)(2,1)S(1)} %collective-permute-done.11), channel_id=1, source_target_pairs={{0,120},{8,0},{16,8},{24,16},{32,24},{40,32},{48,40},{56,48},{64,5... | collective-permute-start | bytes 2359304 | tf_op jit(solution)/shard_map/ppermute | solution.py:69
  151.4 16.0 %collective-permute-start.14 = (bf16[1,1,6,256,256]{4,3,2,1,0:T(8,128)(2,1)S(1)}, bf16[1,1,6,256,256]{4,3,2,1,0:T(8,128)(2,1)S(1)}, u32[]{:S(2)}, u32[]{:S(2)}) collective-permute-start(bf16[1,1,6,256,256]{4,3,2,1,0:T(8,128)(2,1)S(1)} %collective-permute-done.12), channel_id=1, source_target_pairs={{0,8},{8,16},{16,24},{24,32},{32,40},{40,48},{48,56},{56,64},{64,7... | collective-permute-start | bytes 2359304 | tf_op jit(solution)/shard_map/ppermute | solution.py:64
  188.6 1.9 copy-start
  256.3 1.9 copy-start
  324.1 1.9 copy-start
  391.9 1.9 copy-start
  464.3 97.9 %copy-start.2 = (f32[1,1,6,256,256]{4,3,2,1,0:T(8,128)S(1)}, f32[1,1,6,256,256]{4,3,2,1,0:T(8,128)}, u32[]{:S(2)}) copy-start(f32[1,1,6,256,256]{4,3,2,1,0:T(8,128)} %param.9) | copy-start | bytes 4718596
Sparse Core Ops, SparseCore 0:
  464.4 97.6 reduce-scatter.3
